TPU v7x, 512 devices: a whole 4x8x8 slice. The times are simulated.
512 devices in a mesh: ens: 2 (over core), lat: 32 (over z, x), chan: 8 (over y).
Axes of the slice: x: 4, y: 8, z: 8, core: 2. Of those that a mesh axis runs over, the one named last changes fastest.
Arguments:
- field: bfloat16 [2, 384, 128, 256], P('ens', 'chan', 'lat'), may hold values from -6 to 6
- cotangent: bfloat16 [2, 384, 128, 256], P('ens', 'chan', 'lat'), may hold values from -6 to 6
- spec_weight: float32 [2, 64, 384], P(None, None, 'chan'), may hold values from -8 to 8
- disco_coef: float32 [128, 9], replicated, may hold values from -2 to 2
- disco_weight: float32 [9, 384], P(None, 'chan'), may hold values from -5 to 5
- disco_rows: int32 [128, 9], replicated, may hold values from 0 to 127, as said below
- disco_shift: int32 [128, 9], replicated, may hold values from -8 to 8
- w_hidden: bfloat16 [384, 768], replicated, may hold values from -0.3125 to 0.3125
- w_output: bfloat16 [768, 384], replicated, may hold values from -0.21875 to 0.21875
Outputs:
- grad_field: bfloat16 [2, 384, 128, 256], P('ens', 'chan', 'lat')
- grad_spec_weight: float32 [2, 64, 384], P(None, None, 'chan')
- grad_disco_weight: float32 [9, 384], P(None, 'chan')
- grad_w_hidden: float32 [384, 768], P('lat')
- grad_w_output: float32 [768, 384], P('lat')
Inputs may be any that keep to these rules, and one draw needn't show every extreme that they name: Entry k of row i of disco_rows names a latitude row within 2 rows of i.
All inputs are finite; a program needn't handle non-finite values.
Results may differ from a plain program's by a relative error of at most 0.013.
Values may be sent and summed in bfloat16 or wider, within the bound.
A program may use at most 64 MiB of HBM per device.

v0:
```python
import math
import jax
import jax.numpy as jnp
from jax import lax
from jax.sharding import PartitionSpec as P

HALO = 2
SHIFT = 8
norm_eps = 1e-06
inv_root_two = 0.7071067811865476
inv_root_tau = 0.3989422804014327
highest = lax.Precision.HIGHEST


def padded_2(block, sides, width):
    for axis, dim in sides:
        count = lax.axis_size(axis)
        forward = [(i, i + 1) for i in range(count - 1)]
        backward = [(target, source) for source, target in forward]
        low = lax.ppermute(
            lax.slice_in_dim(block, block.shape[dim] - width, None, axis=dim), axis, forward
        )
        high = lax.ppermute(lax.slice_in_dim(block, 0, width, axis=dim), axis, backward)
        block = jnp.concatenate([low, block, high], axis=dim)
    return block


def colatitudes(lat_count):
    return (jnp.arange(lat_count, dtype=jnp.int32).astype(jnp.float32) + 0.5) * (
        math.pi / lat_count
    )


def legendre_rows(first_order, order_count, lat_count, degree_count):
    colatitude = colatitudes(lat_count)
    cosine = jnp.cos(colatitude)
    sine_rows = jnp.sin(colatitude)
    orders = (first_order + jnp.arange(order_count, dtype=jnp.int32)).astype(jnp.float32)
    log_start = 0.5 * (
        jnp.log((2.0 * orders + 1.0) / (4.0 * math.pi))
        + lax.lgamma(orders + 0.5)
        - lax.lgamma(orders + 1.0)
        - 0.5 * math.log(math.pi)
    )
    diagonal = jnp.exp(log_start[:, None] + orders[:, None] * jnp.log(sine_rows)[None, :])

    def advance(carry, degree):
        previous, before = carry
        degree_value = degree.astype(jnp.float32)
        above = degree_value > orders
        upper_term = jnp.where(above, 4.0 * degree_value * degree_value - 1.0, 1.0)
        lower_term = jnp.where(above, degree_value * degree_value - orders * orders, 1.0)
        factor = jnp.sqrt(upper_term / lower_term)
        behind = jnp.where(
            above, (degree_value - 1.0) * (degree_value - 1.0) - orders * orders, 0.0
        )
        damping = jnp.sqrt(behind / (4.0 * (degree_value - 1.0) * (degree_value - 1.0) - 1.0))
        recurred = factor[:, None] * (cosine[None, :] * previous - damping[:, None] * before)
        current = jnp.where(
            above[:, None], recurred, jnp.where((degree_value == orders)[:, None], diagonal, 0.0)
        )
        return ((current, previous), current)

    zero_rows = jnp.zeros((order_count, lat_count), jnp.float32)
    finish, stacked = lax.scan(
        advance, (zero_rows, zero_rows), jnp.arange(degree_count, dtype=jnp.int32), unroll=True
    )
    return jnp.transpose(stacked, (1, 0, 2))


def quadrature(lat_count, lon_count):
    return 2.0 * math.pi / lon_count * (math.pi / lat_count) * jnp.sin(colatitudes(lat_count))


def lon_tables(lon_count, mode_count):
    columns = jnp.arange(lon_count, dtype=jnp.int32)
    mode_ids = jnp.arange(mode_count, dtype=jnp.int32)
    phase_ids = columns[:, None] * mode_ids[None, :] % lon_count
    angles = phase_ids.astype(jnp.float32) * (2.0 * math.pi / lon_count)
    cosine = jnp.cos(angles)
    sine_part = jnp.sin(angles)
    forward = jnp.concatenate([cosine, -sine_part], axis=1).astype(jnp.bfloat16)
    doubled = jnp.where(mode_ids == 0, 1.0, 2.0).astype(jnp.float32)[None, :]
    inverse = jnp.transpose(
        jnp.concatenate([doubled * cosine, -doubled * sine_part], axis=1)
    ).astype(jnp.bfloat16)
    return (forward, inverse)


def apply_filter(coeffs, spec_weight):
    real_weight = jnp.transpose(spec_weight[0])[:, None, :]
    imag_weight = jnp.transpose(spec_weight[1])[:, None, :]
    real_part = coeffs[:, 0]
    imag_part = coeffs[:, 1]
    return jnp.stack(
        [
            real_weight * real_part - imag_weight * imag_part,
            real_weight * imag_part + imag_weight * real_part,
        ],
        axis=1,
    )


def filter_adjoint(grads, coeffs, spec_weight):
    real_weight = jnp.transpose(spec_weight[0])[:, None, :]
    imag_weight = jnp.transpose(spec_weight[1])[:, None, :]
    grad_real = grads[:, 0]
    grad_imag = grads[:, 1]
    real_part = coeffs[:, 0]
    imag_part = coeffs[:, 1]
    weight_zero = jnp.transpose(jnp.sum(grad_real * real_part + grad_imag * imag_part, axis=1))
    weight_one = jnp.transpose(jnp.sum(grad_imag * real_part - grad_real * imag_part, axis=1))
    adjoint_coeffs = jnp.stack(
        [
            real_weight * grad_real + imag_weight * grad_imag,
            real_weight * grad_imag - imag_weight * grad_real,
        ],
        axis=1,
    )
    return (adjoint_coeffs, jnp.stack([weight_zero, weight_one], axis=0))


def mlp_backward(mixed_rows, adjoint_rows, w_hidden, w_output):
    mixed32 = mixed_rows.astype(jnp.float32)
    rscale = lax.rsqrt(jnp.mean(mixed32 * mixed32, axis=0, keepdims=True) + norm_eps)
    normed32 = mixed32 * rscale
    normed = normed32.astype(jnp.bfloat16)
    preact = lax.dot_general(
        w_hidden, normed, (((0,), (0,)), ((), ())), preferred_element_type=jnp.float32
    )
    activated = jax.nn.gelu(preact, approximate=False).astype(jnp.bfloat16)
    grad_output = lax.dot_general(
        activated, adjoint_rows, (((1,), (1,)), ((), ())), preferred_element_type=jnp.float32
    )
    grad_act = lax.dot_general(
        w_output, adjoint_rows, (((1,), (0,)), ((), ())), preferred_element_type=jnp.float32
    )
    cumulative = 0.5 * (1.0 + lax.erf(preact * inv_root_two))
    density = jnp.exp(-0.5 * preact * preact) * inv_root_tau
    grad_pre = (grad_act * (cumulative + preact * density)).astype(jnp.bfloat16)
    grad_hidden = lax.dot_general(
        normed, grad_pre, (((1,), (1,)), ((), ())), preferred_element_type=jnp.float32
    )
    grad_normed = lax.dot_general(
        w_hidden, grad_pre, (((1,), (0,)), ((), ())), preferred_element_type=jnp.float32
    )
    grad_mixed = (
        rscale * (grad_normed - normed32 * jnp.mean(grad_normed * normed32, axis=0, keepdims=True))
    ).astype(jnp.bfloat16)
    return (grad_mixed, grad_hidden, grad_output)


def to_modes(spectrum):
    return lax.all_to_all(spectrum, "lat", split_axis=3, concat_axis=1, tiled=True)


def to_bands(spectrum):
    return lax.all_to_all(spectrum, "lat", split_axis=1, concat_axis=3, tiled=True)


def wrap_lon(values, width):
    return jnp.concatenate([values[:, :, -width:], values, values[:, :, :width]], axis=2)


def disco_kernel(rows_tab, shift_tab, coef_tab, centre, disco_weight):
    row_step = rows_tab - centre[:, None] + HALO
    lon_step = shift_tab + SHIFT
    reach = jnp.arange(2 * HALO + 1, dtype=jnp.int32)
    span = jnp.arange(2 * SHIFT + 1, dtype=jnp.int32)
    onehot = (
        (row_step[:, :, None, None] == reach[None, None, :, None])
        & (lon_step[:, :, None, None] == span[None, None, None, :])
    ).astype(jnp.float32)
    kernel = jnp.einsum("rk,rkpq,kc->crpq", coef_tab, onehot, disco_weight, precision=highest)
    return (onehot, kernel)


def shards(
    field,
    cotangent,
    spec_weight,
    disco_coef,
    disco_weight,
    disco_rows,
    disco_shift,
    w_hidden,
    w_output,
):
    member = field[0]
    adjoint_member = cotangent[0]
    channels, lat_rows, lon_count = member.shape
    band_count = lax.axis_size("lat")
    lat_count = lat_rows * band_count
    mode_count = lat_count // 2
    modes_here = mode_count // band_count
    band_index = lax.axis_index("lat")
    first_row = band_index * lat_rows
    forward, inverse = lon_tables(lon_count, mode_count)
    legendre = legendre_rows(band_index * modes_here, modes_here, lat_count, mode_count)
    weighted = legendre * quadrature(lat_count, lon_count)[None, None, :]
    grad_scale = 1.0 / math.sqrt(lax.axis_size("ens") * lat_count * lon_count)
    reach_count = 2 * HALO + 1
    span_count = 2 * SHIFT + 1
    adjoint_rows = lax.all_to_all(adjoint_member, "chan", split_axis=2, concat_axis=0, tiled=True)
    spectrum = jnp.dot(
        member.reshape(channels * lat_rows, lon_count), forward, preferred_element_type=jnp.float32
    )
    spectrum = spectrum.astype(jnp.bfloat16).reshape(channels, lat_rows, 2, mode_count)
    mode_block = to_modes(spectrum)
    coeffs = jnp.einsum(
        "citm,mli->ctml", mode_block.astype(jnp.float32), weighted, precision=highest
    )
    synthesis = jnp.einsum(
        "ctml,mli->citm", apply_filter(coeffs, spec_weight), legendre, precision=highest
    ).astype(jnp.bfloat16)
    band_block = to_bands(synthesis)
    spectral = jnp.dot(
        band_block.reshape(channels * lat_rows, 2 * mode_count),
        inverse,
        preferred_element_type=jnp.float32,
    )
    spectral = spectral.reshape(channels, lat_rows, lon_count)
    global_rows = first_row + jnp.arange(lat_rows, dtype=jnp.int32)
    rows_here = lax.dynamic_slice_in_dim(disco_rows, first_row, lat_rows, 0)
    shift_here = lax.dynamic_slice_in_dim(disco_shift, first_row, lat_rows, 0)
    coef_here = lax.dynamic_slice_in_dim(disco_coef, first_row, lat_rows, 0)
    onehot_here, kernel_here = disco_kernel(
        rows_here, shift_here, coef_here, global_rows, disco_weight
    )
    padded = padded_2(member, (("lat", 1),), HALO)
    wide_field = wrap_lon(padded, SHIFT)
    disco_out = jnp.zeros((channels, lat_rows, lon_count), jnp.float32)
    for reach in range(reach_count):
        for span in range(span_count):
            window = wide_field[:, reach : reach + lat_rows, span : span + lon_count].astype(
                jnp.float32
            )
            disco_out = disco_out + kernel_here[:, :, reach, span][:, :, None] * window
    mixed_field = (spectral + disco_out).astype(jnp.bfloat16)
    mixed_rows = lax.all_to_all(mixed_field, "chan", split_axis=2, concat_axis=0, tiled=True)
    all_channels = mixed_rows.shape[0]
    row_width = mixed_rows.shape[2]
    grad_rows, grad_hidden, grad_output = mlp_backward(
        mixed_rows.reshape(all_channels, lat_rows * row_width),
        adjoint_rows.reshape(all_channels, lat_rows * row_width),
        w_hidden,
        w_output,
    )
    grad_field = lax.all_to_all(
        grad_rows.reshape(all_channels, lat_rows, row_width),
        "chan",
        split_axis=0,
        concat_axis=2,
        tiled=True,
    )
    grad_synth = lax.dot_general(
        grad_field.reshape(channels * lat_rows, lon_count),
        inverse,
        (((1,), (1,)), ((), ())),
        preferred_element_type=jnp.float32,
    )
    grad_synth = grad_synth.astype(jnp.bfloat16).reshape(channels, lat_rows, 2, mode_count)
    grad_modes = to_modes(grad_synth)
    grad_filtered = jnp.einsum(
        "citm,mli->ctml", grad_modes.astype(jnp.float32), legendre, precision=highest
    )
    grad_coeffs, filter_part = filter_adjoint(grad_filtered, coeffs, spec_weight)
    grad_spectrum = jnp.einsum("ctml,mli->citm", grad_coeffs, weighted, precision=highest).astype(
        jnp.bfloat16
    )
    grad_lines = to_bands(grad_spectrum)
    spectral_back = lax.dot_general(
        grad_lines.reshape(channels * lat_rows, 2 * mode_count),
        forward,
        (((1,), (1,)), ((), ())),
        preferred_element_type=jnp.float32,
    )
    spectral_back = spectral_back.reshape(channels, lat_rows, lon_count)
    grad_wide = grad_field.astype(jnp.float32)
    reach_sums = []
    for reach in range(reach_count):
        span_sums = []
        for span in range(span_count):
            window = wide_field[:, reach : reach + lat_rows, span : span + lon_count].astype(
                jnp.float32
            )
            span_sums.append(jnp.sum(window * grad_wide, axis=2))
        reach_sums.append(jnp.stack(span_sums, axis=2))
    inner_sum = jnp.stack(reach_sums, axis=2)
    disco_part = jnp.einsum(
        "ik,ikpq,cipq->kc", coef_here, onehot_here, inner_sum, precision=highest
    )
    rimmed = padded_2(grad_field, (("lat", 1),), HALO)
    wide_grads = wrap_lon(rimmed, SHIFT)
    ext_count = lat_rows + 2 * HALO
    ext_rows = first_row - HALO + jnp.arange(ext_count, dtype=jnp.int32)
    rows_ext = lax.dynamic_slice_in_dim(
        jnp.pad(disco_rows, ((HALO, HALO), (0, 0))), first_row, ext_count, 0
    )
    shift_ext = lax.dynamic_slice_in_dim(
        jnp.pad(disco_shift, ((HALO, HALO), (0, 0))), first_row, ext_count, 0
    )
    coef_ext = lax.dynamic_slice_in_dim(
        jnp.pad(disco_coef, ((HALO, HALO), (0, 0))), first_row, ext_count, 0
    )
    onehot_ext, kernel_ext = disco_kernel(rows_ext, shift_ext, coef_ext, ext_rows, disco_weight)
    spread = jnp.zeros((channels, lat_rows, lon_count), jnp.float32)
    for reach in range(reach_count):
        row_start = 2 * HALO - reach
        for span in range(span_count):
            col_start = 2 * SHIFT - span
            window = wide_grads[
                :, row_start : row_start + lat_rows, col_start : col_start + lon_count
            ].astype(jnp.float32)
            spread = (
                spread
                + kernel_ext[:, row_start : row_start + lat_rows, reach, span][:, :, None] * window
            )
    grad_input = (adjoint_member.astype(jnp.float32) + spectral_back + spread).astype(jnp.bfloat16)
    filter_total, disco_total = lax.psum((filter_part, disco_part), ("ens", "lat"))
    total_hidden, total_output = lax.psum((grad_hidden, grad_output), ("ens", "lat", "chan"))
    hidden_rows = total_hidden.shape[0] // band_count
    output_rows = total_output.shape[0] // band_count
    share_hidden = lax.dynamic_slice_in_dim(total_hidden, band_index * hidden_rows, hidden_rows, 0)
    share_output = lax.dynamic_slice_in_dim(total_output, band_index * output_rows, output_rows, 0)
    return (
        grad_input[None],
        filter_total,
        disco_total * grad_scale,
        share_hidden * grad_scale,
        share_output * grad_scale,
    )


def solution(mesh):
    in_specs = (
        P("ens", "chan", "lat", None),
        P("ens", "chan", "lat", None),
        P(None, None, "chan"),
        P(),
        P(None, "chan"),
        P(),
        P(),
        P(),
        P(),
    )
    out_specs = (
        P("ens", "chan", "lat", None),
        P(None, None, "chan"),
        P(None, "chan"),
        P("lat", None),
        P("lat", None),
    )
    return jax.shard_map(shards, mesh=mesh, in_specs=in_specs, out_specs=out_specs, check_vma=False)
```

profile of v0, /device:TPU:256, one launch (start us, length us, event | category | flops | bytes accessed | tf_op | source)
XLA Modules:
  0.0 485.7 jit_solution(5748793667730272015)
XLA Ops:
  7.5 0.9 reshape_squeeze.3
  8.9 0.8 reshape.55196
  9.7 9.9 %all-to-all-start = ((bf16[32,2,384]{2,1,0:T(2,128)(2,1)}), bf16[32,2,384]{2,1,0:T(2,128)(2,1)S(1)}, u32[]{:S(2)}, u32[]{:S(2)}) async-start(bf16[32,2,384]{2,1,0:T(2,128)(2,1)} %reshape.55196), calls=%async_computation | async-start | bytes 98304 | tf_op jit(solution)/shard_map/all_to_all | solution.py:154
  19.6 3.4 collective-permute-start
  23.0 5.8 %collective-permute-start.1 = (bf16[48,2,256]{2,0,1:T(8,128)(2,1)S(1)}, bf16[48,2,256]{2,0,1:T(8,128)(2,1)S(1)}, u32[]{:S(2)}, u32[]{:S(2)}) collective-permute-start(bf16[48,2,256]{2,0,1:T(8,128)(2,1)S(1)} %get-tuple-element.536), channel_id=1, source_target_pairs={{8,0},{16,8},{24,16},{32,24},{40,32},{48,40},{56,48},{64,56},{72,6... | collective-permute-start | bytes 147464 | tf_op jit(solution)/shard_map/ppermute | solution.py:23
  28.8 0.7 fusion.693
  33.5 0.7 fusion.694
  45.7 0.7 fusion.695
  50.4 0.7 fusion.692
  74.1 0.6 fusion.684
  74.7 0.7 fusion.685
  75.4 0.7 fusion.686
  77.1 0.9 convolution_bitcast_fusion
  78.7 0.7 fusion.681
  85.0 1.0 reshape.55202
  86.0 0.7 copy.394
  88.0 0.8 reshape.55198
  89.2 7.4 %all-to-all-start.1 = ((bf16[32,2,384]{2,1,0:T(2,128)(2,1)}), bf16[32,2,384]{2,1,0:T(2,128)(2,1)S(1)}, u32[]{:S(2)}, u32[]{:S(2)}) async-start(bf16[32,2,384]{2,1,0:T(2,128)(2,1)} %reshape.55198), calls=%async_computation.1 | async-start | bytes 98304 | tf_op jit(solution)/shard_map/all_to_all | solution.py:158
  96.8 4.9 %all-to-all-done.1 = bf16[32,2,384]{2,1,0:T(2,128)(2,1)S(1)} async-done(((bf16[32,2,384]{2,1,0:T(2,128)(2,1)}), bf16[32,2,384]{2,1,0:T(2,128)(2,1)S(1)}, u32[]{:S(2)}, u32[]{:S(2)}) %all-to-all-start.1) | async-done | bytes 49184 | tf_op jit(solution)/shard_map/all_to_all | solution.py:158
  101.7 7.1 %all-to-all-start.3 = ((bf16[8,2,3072]{2,1,0:T(2,128)(2,1)}), bf16[8,2,3072]{2,1,0:T(2,128)(2,1)S(1)}, u32[]{:S(2)}, u32[]{:S(2)}) async-start(bf16[8,2,3072]{2,1,0:T(2,128)(2,1)} %reshape.55202), calls=%async_computation.3 | async-start | bytes 196608 | tf_op jit(solution)/shard_map/all_to_all | solution.py:204
  109.5 6.0 %fusion.2 = bf16[48,4,256]{2,0,1:T(8,128)(2,1)S(1)} fusion(bf16[48,4,128]{0,2,1:T(8,128)(2,1)S(1)} %bitcast.623, bf16[48,4,256]{2,0,1:T(8,128)(2,1)S(1)} %bitcast.596, f32[48,4]{0,1:T(4,128)S(1)} %bitcast.820, f32[48,4]{0,1:T(4,128)S(1)} %bitcast.821, f32[48,4]{0,1:T(4,128)S(1)} %bitcast.822, f32[48,4]{0,1:T(4,128)S(1)} %bitcast.823, ...), kind=kOutput, calls=%fused_computation.173 | convolution fusion | flops 25493504 | bytes 8339200 | tf_op jit(solution)/shard_map/dot_general | solution.py:217
  115.7 1.0 reshape.55200
  116.7 0.8 all-to-all-done.3
  117.6 6.4 %all-to-all-start.2 = ((bf16[8,2,3072]{2,1,0:T(2,128)(2,1)}), bf16[8,2,3072]{2,1,0:T(2,128)(2,1)S(1)}, u32[]{:S(2)}, u32[]{:S(2)}) async-start(bf16[8,2,3072]{2,1,0:T(2,128)(2,1)} %reshape.55200), calls=%async_computation.2 | async-start | bytes 196608 | tf_op jit(solution)/shard_map/all_to_all | solution.py:240
  123.9 0.6 fusion.682
  125.2 7.5 %all-to-all-done.2 = bf16[8,2,3072]{2,1,0:T(2,128)(2,1)S(1)} async-done(((bf16[8,2,3072]{2,1,0:T(2,128)(2,1)}), bf16[8,2,3072]{2,1,0:T(2,128)(2,1)S(1)}, u32[]{:S(2)}, u32[]{:S(2)}) %all-to-all-start.2) | async-done | bytes 98336 | tf_op jit(solution)/shard_map/all_to_all | solution.py:240
  134.6 2.0 fusion.24
  137.8 1.0 reshape.55204
  138.8 3.4 all-to-all-start.4
  142.5 1.5 fusion.613
  144.0 6.9 %all-to-all-done.4 = bf16[8,2,3072]{2,1,0:T(2,128)(2,1)S(1)} async-done(((bf16[8,2,3072]{2,1,0:T(2,128)(2,1)}), bf16[8,2,3072]{2,1,0:T(2,128)(2,1)S(1)}, u32[]{:S(2)}, u32[]{:S(2)}) %all-to-all-start.4) | async-done | bytes 98336 | tf_op jit(solution)/shard_map/all_to_all | solution.py:249
  152.1 1.1 fusion.210
  153.2 1.2 fusion.219
  154.4 1.1 fusion.209
  155.5 1.2 fusion.218
  157.4 0.8 reshape.55206
  158.3 8.6 %all-to-all-start.5 = ((bf16[32,2,384]{2,1,0:T(2,128)(2,1)}), bf16[32,2,384]{2,1,0:T(2,128)(2,1)S(1)}, u32[]{:S(2)}, u32[]{:S(2)}) async-start(bf16[32,2,384]{2,1,0:T(2,128)(2,1)} %reshape.55206), calls=%async_computation.5 | async-start | bytes 98304 | tf_op jit(solution)/shard_map/all_to_all | solution.py:154
  166.9 3.4 collective-permute-start.2
  170.3 5.8 %collective-permute-start.3 = (bf16[48,2,256]{2,0,1:T(8,128)(2,1)S(1)}, bf16[48,2,256]{2,0,1:T(8,128)(2,1)S(1)}, u32[]{:S(2)}, u32[]{:S(2)}) collective-permute-start(bf16[48,2,256]{2,0,1:T(8,128)(2,1)S(1)} %get-tuple-element.534), channel_id=1, source_target_pairs={{8,0},{16,8},{24,16},{32,24},{40,32},{48,40},{56,48},{64,56},{72,6... | collective-permute-start | bytes 147464 | tf_op jit(solution)/shard_map/ppermute | solution.py:23
  176.1 0.8 fusion.217
  177.3 0.7 convolution_bitcast_fusion.6
  179.5 0.8 reshape.55208
  180.3 10.2 %all-to-all-start.6 = ((bf16[32,2,384]{2,1,0:T(2,128)(2,1)}), bf16[32,2,384]{2,1,0:T(2,128)(2,1)S(1)}, u32[]{:S(2)}, u32[]{:S(2)}) async-start(bf16[32,2,384]{2,1,0:T(2,128)(2,1)} %reshape.55208), calls=%async_computation.6 | async-start | bytes 98304 | tf_op jit(solution)/shard_map/all_to_all | solution.py:158
  190.5 276.9 %all-reduce.4 = (f32[2,64,48]{1,2,0:T(8,128)}, f32[9,48]{1,0:T(8,128)S(1)}) all-reduce(f32[2,64,48]{1,2,0:T(8,128)S(1)} %pad_maximum_fusion.8, f32[9,48]{1,0:T(8,128)S(1)} %convolution_bitcast_fusion.6), channel_id=1, replica_groups=mesh['ens'=2,'lat'=32,'chan'=8] {'ens','lat'}, use_global_device_ids=true, to_apply=%region_5.6 | all-reduce | flops 6576 | bytes 52608 | tf_op jit(solution)/shard_map/psum | solution.py:320
  468.7 6.5 %fusion.4 = bf16[1,48,4,256]{3,1,2,0:T(8,128)(2,1)S(1)} fusion(bf16[48,4,128]{0,2,1:T(8,128)(2,1)S(1)} %bitcast.622, bf16[48,4,256]{2,0,1:T(8,128)(2,1)S(1)} %all_to_all.100, bf16[48,8,256]{2,0,1:T(8,128)(2,1)S(1)} %get-tuple-element.539, bf16[48,8,8]{2,0,1:T(8,128)(2,1)S(1)} %get-tuple-element.520, bf16[48,8,8]{2,0,1:T(8,128)(2,1)S(1)} %get-tuple-element.519, ...), kind=kOutput, calls=%fused_computation.177 | convolution fusion | flops 37191680 | bytes 1076992 | tf_op jit(solution)/shard_map/dot_general | solution.py:272
  475.2 0.7 copy.395
  475.9 1.5 dynamic-slice_multiply_fusion
  477.5 1.4 dynamic-slice_multiply_fusion.1
  (425 shorter events, 18.6 us)
Async XLA Ops:
  7.2 127.0 %copy-start = (bf16[384,768]{1,0:T(8,128)(2,1)S(1)}, bf16[384,768]{1,0:T(8,128)(2,1)}, u32[]{:S(2)}) copy-start(bf16[384,768]{1,0:T(8,128)(2,1)} %param.16) | copy-start | bytes 1769476
  8.6 64.8 %copy-start.82 = (f32[9,48]{1,0:T(8,128)S(1)}, f32[9,48]{1,0:T(8,128)}, u32[]{:S(2)}) copy-start(f32[9,48]{1,0:T(8,128)} %param.13) | copy-start | bytes 5188
  9.7 77.4 %all-to-all-start = ((bf16[32,2,384]{2,1,0:T(2,128)(2,1)}), bf16[32,2,384]{2,1,0:T(2,128)(2,1)S(1)}, u32[]{:S(2)}, u32[]{:S(2)}) async-start(bf16[32,2,384]{2,1,0:T(2,128)(2,1)} %reshape.55196), calls=%async_computation | async-start | bytes 98304 | tf_op jit(solution)/shard_map/all_to_all | solution.py:154
  19.6 67.3 %collective-permute-start = (bf16[48,2,256]{2,0,1:T(8,128)(2,1)S(1)}, bf16[48,2,256]{2,0,1:T(8,128)(2,1)S(1)}, u32[]{:S(2)}, u32[]{:S(2)}) collective-permute-start(bf16[48,2,256]{2,0,1:T(8,128)(2,1)S(1)} %get-tuple-element.537), channel_id=1, source_target_pairs={{0,8},{8,16},{16,24},{24,32},{32,40},{40,48},{48,56},{56,64},{64,7... | collective-permute-start | bytes 147464 | tf_op jit(solution)/shard_map/ppermute | solution.py:20
  23.0 63.9 %collective-permute-start.1 = (bf16[48,2,256]{2,0,1:T(8,128)(2,1)S(1)}, bf16[48,2,256]{2,0,1:T(8,128)(2,1)S(1)}, u32[]{:S(2)}, u32[]{:S(2)}) collective-permute-start(bf16[48,2,256]{2,0,1:T(8,128)(2,1)S(1)} %get-tuple-element.536), channel_id=1, source_target_pairs={{8,0},{16,8},{24,16},{32,24},{40,32},{48,40},{56,48},{64,56},{72,6... | collective-permute-start | bytes 147464 | tf_op jit(solution)/shard_map/ppermute | solution.py:23
  89.2 12.5 %all-to-all-start.1 = ((bf16[32,2,384]{2,1,0:T(2,128)(2,1)}), bf16[32,2,384]{2,1,0:T(2,128)(2,1)S(1)}, u32[]{:S(2)}, u32[]{:S(2)}) async-start(bf16[32,2,384]{2,1,0:T(2,128)(2,1)} %reshape.55198), calls=%async_computation.1 | async-start | bytes 98304 | tf_op jit(solution)/shard_map/all_to_all | solution.py:158
  101.7 15.8 %all-to-all-start.3 = ((bf16[8,2,3072]{2,1,0:T(2,128)(2,1)}), bf16[8,2,3072]{2,1,0:T(2,128)(2,1)S(1)}, u32[]{:S(2)}, u32[]{:S(2)}) async-start(bf16[8,2,3072]{2,1,0:T(2,128)(2,1)} %reshape.55202), calls=%async_computation.3 | async-start | bytes 196608 | tf_op jit(solution)/shard_map/all_to_all | solution.py:204
  117.6 15.1 %all-to-all-start.2 = ((bf16[8,2,3072]{2,1,0:T(2,128)(2,1)}), bf16[8,2,3072]{2,1,0:T(2,128)(2,1)S(1)}, u32[]{:S(2)}, u32[]{:S(2)}) async-start(bf16[8,2,3072]{2,1,0:T(2,128)(2,1)} %reshape.55200), calls=%async_computation.2 | async-start | bytes 196608 | tf_op jit(solution)/shard_map/all_to_all | solution.py:240
  138.8 12.0 %all-to-all-start.4 = ((bf16[8,2,3072]{2,1,0:T(2,128)(2,1)}), bf16[8,2,3072]{2,1,0:T(2,128)(2,1)S(1)}, u32[]{:S(2)}, u32[]{:S(2)}) async-start(bf16[8,2,3072]{2,1,0:T(2,128)(2,1)} %reshape.55204), calls=%async_computation.4 | async-start | bytes 196608 | tf_op jit(solution)/shard_map/all_to_all | solution.py:249
  142.2 333.7 %all-reduce.7.cloned.1.call-start = ((), (), s32[]{:S(2)}) async-start(), calls=%async_computation.7 | async-start | bytes 4718592 | tf_op jit(solution)/shard_map/psum | solution.py:321
  158.3 19.9 %all-to-all-start.5 = ((bf16[32,2,384]{2,1,0:T(2,128)(2,1)}), bf16[32,2,384]{2,1,0:T(2,128)(2,1)S(1)}, u32[]{:S(2)}, u32[]{:S(2)}) async-start(bf16[32,2,384]{2,1,0:T(2,128)(2,1)} %reshape.55206), calls=%async_computation.5 | async-start | bytes 98304 | tf_op jit(solution)/shard_map/all_to_all | solution.py:154
  166.9 11.1 %collective-permute-start.2 = (bf16[48,2,256]{2,0,1:T(8,128)(2,1)S(1)}, bf16[48,2,256]{2,0,1:T(8,128)(2,1)S(1)}, u32[]{:S(2)}, u32[]{:S(2)}) collective-permute-start(bf16[48,2,256]{2,0,1:T(8,128)(2,1)S(1)} %get-tuple-element.535), channel_id=1, source_target_pairs={{0,8},{8,16},{16,24},{24,32},{32,40},{40,48},{48,56},{56,64},{64,7... | collective-permute-start | bytes 147464 | tf_op jit(solution)/shard_map/ppermute | solution.py:20
  170.3 7.8 %collective-permute-start.3 = (bf16[48,2,256]{2,0,1:T(8,128)(2,1)S(1)}, bf16[48,2,256]{2,0,1:T(8,128)(2,1)S(1)}, u32[]{:S(2)}, u32[]{:S(2)}) collective-permute-start(bf16[48,2,256]{2,0,1:T(8,128)(2,1)S(1)} %get-tuple-element.534), channel_id=1, source_target_pairs={{8,0},{16,8},{24,16},{32,24},{40,32},{48,40},{56,48},{64,56},{72,6... | collective-permute-start | bytes 147464 | tf_op jit(solution)/shard_map/ppermute | solution.py:23
  178.8 289.6 %copy-start.7 = (f32[48,4,1,1]{0,3,2,1:T(1,128)S(1)}, f32[48,4,1,1]{0,3,2,1:T(1,128)}, u32[]{:S(2)}) copy-start(f32[48,4,1,1]{0,3,2,1:T(1,128)} %get-tuple-element.400) | copy-start | bytes 2308
  178.8 289.6 %copy-start.8 = (f32[48,4,1,1]{0,3,2,1:T(1,128)S(1)}, f32[48,4,1,1]{0,3,2,1:T(1,128)}, u32[]{:S(2)}) copy-start(f32[48,4,1,1]{0,3,2,1:T(1,128)} %get-tuple-element.401) | copy-start | bytes 2308
  178.8 289.6 %copy-start.9 = (f32[48,4,1,1]{0,3,2,1:T(1,128)S(1)}, f32[48,4,1,1]{0,3,2,1:T(1,128)}, u32[]{:S(2)}) copy-start(f32[48,4,1,1]{0,3,2,1:T(1,128)} %get-tuple-element.402) | copy-start | bytes 2308
  178.8 289.6 %copy-start.10 = (f32[48,4,1,1]{0,3,2,1:T(1,128)S(1)}, f32[48,4,1,1]{0,3,2,1:T(1,128)}, u32[]{:S(2)}) copy-start(f32[48,4,1,1]{0,3,2,1:T(1,128)} %get-tuple-element.403) | copy-start | bytes 2308
  178.8 289.6 %copy-start.11 = (f32[48,4,1,1]{0,3,2,1:T(1,128)S(1)}, f32[48,4,1,1]{0,3,2,1:T(1,128)}, u32[]{:S(2)}) copy-start(f32[48,4,1,1]{0,3,2,1:T(1,128)} %get-tuple-element.404) | copy-start | bytes 2308
  178.8 289.6 %copy-start.12 = (f32[48,4,1,1]{0,3,2,1:T(1,128)S(1)}, f32[48,4,1,1]{0,3,2,1:T(1,128)}, u32[]{:S(2)}) copy-start(f32[48,4,1,1]{0,3,2,1:T(1,128)} %get-tuple-element.405) | copy-start | bytes 2308
  178.8 289.6 %copy-start.13 = (f32[48,4,1,1]{0,3,2,1:T(1,128)S(1)}, f32[48,4,1,1]{0,3,2,1:T(1,128)}, u32[]{:S(2)}) copy-start(f32[48,4,1,1]{0,3,2,1:T(1,128)} %get-tuple-element.406) | copy-start | bytes 2308
  178.8 289.6 %copy-start.14 = (f32[48,4,1,1]{0,3,2,1:T(1,128)S(1)}, f32[48,4,1,1]{0,3,2,1:T(1,128)}, u32[]{:S(2)}) copy-start(f32[48,4,1,1]{0,3,2,1:T(1,128)} %get-tuple-element.407) | copy-start | bytes 2308
  178.9 289.6 %copy-start.15 = (f32[48,4,1,1]{0,3,2,1:T(1,128)S(1)}, f32[48,4,1,1]{0,3,2,1:T(1,128)}, u32[]{:S(2)}) copy-start(f32[48,4,1,1]{0,3,2,1:T(1,128)} %get-tuple-element.408) | copy-start | bytes 2308
  178.9 289.6 %copy-start.16 = (f32[48,4,1,1]{0,3,2,1:T(1,128)S(1)}, f32[48,4,1,1]{0,3,2,1:T(1,128)}, u32[]{:S(2)}) copy-start(f32[48,4,1,1]{0,3,2,1:T(1,128)} %get-tuple-element.409) | copy-start | bytes 2308
  178.9 289.6 %copy-start.17 = (f32[48,4,1,1]{0,3,2,1:T(1,128)S(1)}, f32[48,4,1,1]{0,3,2,1:T(1,128)}, u32[]{:S(2)}) copy-start(f32[48,4,1,1]{0,3,2,1:T(1,128)} %get-tuple-element.410) | copy-start | bytes 2308
  178.9 289.6 %copy-start.18 = (f32[48,4,1,1]{0,3,2,1:T(1,128)S(1)}, f32[48,4,1,1]{0,3,2,1:T(1,128)}, u32[]{:S(2)}) copy-start(f32[48,4,1,1]{0,3,2,1:T(1,128)} %get-tuple-element.411) | copy-start | bytes 2308
  178.9 289.6 %copy-start.19 = (f32[48,4,1,1]{0,3,2,1:T(1,128)S(1)}, f32[48,4,1,1]{0,3,2,1:T(1,128)}, u32[]{:S(2)}) copy-start(f32[48,4,1,1]{0,3,2,1:T(1,128)} %get-tuple-element.412) | copy-start | bytes 2308
  178.9 289.6 %copy-start.20 = (f32[48,4,1,1]{0,3,2,1:T(1,128)S(1)}, f32[48,4,1,1]{0,3,2,1:T(1,128)}, u32[]{:S(2)}) copy-start(f32[48,4,1,1]{0,3,2,1:T(1,128)} %get-tuple-element.413) | copy-start | bytes 2308
  178.9 289.6 %copy-start.21 = (f32[48,4,1,1]{0,3,2,1:T(1,128)S(1)}, f32[48,4,1,1]{0,3,2,1:T(1,128)}, u32[]{:S(2)}) copy-start(f32[48,4,1,1]{0,3,2,1:T(1,128)} %get-tuple-element.414) | copy-start | bytes 2308
  178.9 289.6 %copy-start.22 = (f32[48,4,1,1]{0,3,2,1:T(1,128)S(1)}, f32[48,4,1,1]{0,3,2,1:T(1,128)}, u32[]{:S(2)}) copy-start(f32[48,4,1,1]{0,3,2,1:T(1,128)} %get-tuple-element.415) | copy-start | bytes 2308
  178.9 289.6 %copy-start.23 = (f32[48,4,1,1]{0,3,2,1:T(1,128)S(1)}, f32[48,4,1,1]{0,3,2,1:T(1,128)}, u32[]{:S(2)}) copy-start(f32[48,4,1,1]{0,3,2,1:T(1,128)} %get-tuple-element.416) | copy-start | bytes 2308
  178.9 289.6 %copy-start.24 = (f32[48,4,1,1]{0,3,2,1:T(1,128)S(1)}, f32[48,4,1,1]{0,3,2,1:T(1,128)}, u32[]{:S(2)}) copy-start(f32[48,4,1,1]{0,3,2,1:T(1,128)} %get-tuple-element.417) | copy-start | bytes 2308
  179.0 289.6 %copy-start.25 = (f32[48,4,1,1]{0,3,2,1:T(1,128)S(1)}, f32[48,4,1,1]{0,3,2,1:T(1,128)}, u32[]{:S(2)}) copy-start(f32[48,4,1,1]{0,3,2,1:T(1,128)} %get-tuple-element.418) | copy-start | bytes 2308
  179.0 289.6 %copy-start.26 = (f32[48,4,1,1]{0,3,2,1:T(1,128)S(1)}, f32[48,4,1,1]{0,3,2,1:T(1,128)}, u32[]{:S(2)}) copy-start(f32[48,4,1,1]{0,3,2,1:T(1,128)} %get-tuple-element.419) | copy-start | bytes 2308
  179.0 289.6 %copy-start.27 = (f32[48,4,1,1]{0,3,2,1:T(1,128)S(1)}, f32[48,4,1,1]{0,3,2,1:T(1,128)}, u32[]{:S(2)}) copy-start(f32[48,4,1,1]{0,3,2,1:T(1,128)} %get-tuple-element.420) | copy-start | bytes 2308
  179.0 289.6 %copy-start.28 = (f32[48,4,1,1]{0,3,2,1:T(1,128)S(1)}, f32[48,4,1,1]{0,3,2,1:T(1,128)}, u32[]{:S(2)}) copy-start(f32[48,4,1,1]{0,3,2,1:T(1,128)} %get-tuple-element.421) | copy-start | bytes 2308
  179.0 289.6 %copy-start.29 = (f32[48,4,1,1]{0,3,2,1:T(1,128)S(1)}, f32[48,4,1,1]{0,3,2,1:T(1,128)}, u32[]{:S(2)}) copy-start(f32[48,4,1,1]{0,3,2,1:T(1,128)} %get-tuple-element.422) | copy-start | bytes 2308
  179.0 289.6 %copy-start.30 = (f32[48,4,1,1]{0,3,2,1:T(1,128)S(1)}, f32[48,4,1,1]{0,3,2,1:T(1,128)}, u32[]{:S(2)}) copy-start(f32[48,4,1,1]{0,3,2,1:T(1,128)} %get-tuple-element.423) | copy-start | bytes 2308
  179.0 289.6 %copy-start.31 = (f32[48,4,1,1]{0,3,2,1:T(1,128)S(1)}, f32[48,4,1,1]{0,3,2,1:T(1,128)}, u32[]{:S(2)}) copy-start(f32[48,4,1,1]{0,3,2,1:T(1,128)} %get-tuple-element.424) | copy-start | bytes 2308
  179.0 289.6 %copy-start.72 = (f32[48,4,1,1]{0,3,2,1:T(1,128)S(1)}, f32[48,4,1,1]{0,3,2,1:T(1,128)}, u32[]{:S(2)}) copy-start(f32[48,4,1,1]{0,3,2,1:T(1,128)} %get-tuple-element.425) | copy-start | bytes 2308
  179.0 289.6 %copy-start.73 = (f32[48,4,1,1]{0,3,2,1:T(1,128)S(1)}, f32[48,4,1,1]{0,3,2,1:T(1,128)}, u32[]{:S(2)}) copy-start(f32[48,4,1,1]{0,3,2,1:T(1,128)} %get-tuple-element.426) | copy-start | bytes 2308
  179.0 289.6 %copy-start.74 = (f32[48,4,1,1]{0,3,2,1:T(1,128)S(1)}, f32[48,4,1,1]{0,3,2,1:T(1,128)}, u32[]{:S(2)}) copy-start(f32[48,4,1,1]{0,3,2,1:T(1,128)} %get-tuple-element.427) | copy-start | bytes 2308
  179.1 289.6 %copy-start.75 = (f32[48,4,1,1]{0,3,2,1:T(1,128)S(1)}, f32[48,4,1,1]{0,3,2,1:T(1,128)}, u32[]{:S(2)}) copy-start(f32[48,4,1,1]{0,3,2,1:T(1,128)} %get-tuple-element.428) | copy-start | bytes 2308
  179.1 289.6 %copy-start.76 = (f32[48,4,1,1]{0,3,2,1:T(1,128)S(1)}, f32[48,4,1,1]{0,3,2,1:T(1,128)}, u32[]{:S(2)}) copy-start(f32[48,4,1,1]{0,3,2,1:T(1,128)} %get-tuple-element.429) | copy-start | bytes 2308
  179.1 289.6 %copy-start.77 = (f32[48,4,1,1]{0,3,2,1:T(1,128)S(1)}, f32[48,4,1,1]{0,3,2,1:T(1,128)}, u32[]{:S(2)}) copy-start(f32[48,4,1,1]{0,3,2,1:T(1,128)} %get-tuple-element.430) | copy-start | bytes 2308
  179.1 289.6 %copy-start.78 = (f32[48,4,1,1]{0,3,2,1:T(1,128)S(1)}, f32[48,4,1,1]{0,3,2,1:T(1,128)}, u32[]{:S(2)}) copy-start(f32[48,4,1,1]{0,3,2,1:T(1,128)} %get-tuple-element.431) | copy-start | bytes 2308
  179.1 289.6 %copy-start.79 = (f32[48,4,1,1]{0,3,2,1:T(1,128)S(1)}, f32[48,4,1,1]{0,3,2,1:T(1,128)}, u32[]{:S(2)}) copy-start(f32[48,4,1,1]{0,3,2,1:T(1,128)} %get-tuple-element.432) | copy-start | bytes 2308
  179.1 289.6 %copy-start.80 = (f32[48,4,1,1]{0,3,2,1:T(1,128)S(1)}, f32[48,4,1,1]{0,3,2,1:T(1,128)}, u32[]{:S(2)}) copy-start(f32[48,4,1,1]{0,3,2,1:T(1,128)} %get-tuple-element.433) | copy-start | bytes 2308
  180.3 287.7 %all-to-all-start.6 = ((bf16[32,2,384]{2,1,0:T(2,128)(2,1)}), bf16[32,2,384]{2,1,0:T(2,128)(2,1)S(1)}, u32[]{:S(2)}, u32[]{:S(2)}) async-start(bf16[32,2,384]{2,1,0:T(2,128)(2,1)} %reshape.55208), calls=%async_computation.6 | async-start | bytes 98304 | tf_op jit(solution)/shard_map/all_to_all | solution.py:158
  (47 other events, 1021.5 us)
Sparse Core Ops, SparseCore 0:
  148.1 279.6 all-reduce.6
where the time goes:
time: 487 us; the launch traced here: 486 us
  blocking collectives  277 us (57%)
  starting transfers between devices  71.5 us (15%)
  between operations  58.2 us (12%)
  local copies, waits for them, and re-layouts  24.1 us (5%)
  matrix products  20.6 us (4%)
  waiting for transfers between devices  20.2 us (4%)
  other arithmetic  14.3 us (3%)
    psum x1, blocking collectives, shards(): lax.psum((filter_part, disco_part), ('ens', 'lat'))  277 us
    all_to_all x2, starting transfers between devices, to_modes(): lax.all_to_all(spectrum, 'lat', split_axis=3, concat_axis=1, tiled=True)  18.5 us
    all_to_all x2, starting transfers between devices, to_bands(): lax.all_to_all(spectrum, 'lat', split_axis=1, concat_axis=3, tiled=True)  17.6 us
    ppermute x2, starting transfers between devices, padded_2(): lax.ppermute(lax.slice_in_dim(block, 0, width, axis=dim), axis, backward)  11.6 us
  transfers between devices with their start and end apart: 12, of which 4 were waited for; matrix products, arithmetic and copies ran while one was open for 9% of the time, Pallas kernels for 0%

commit v1 on v0

--- a/solution.py
+++ b/solution.py
@@ -10,6 +10,29 @@
 inv_root_two = 0.7071067811865476
 inv_root_tau = 0.3989422804014327
 highest = lax.Precision.HIGHEST
+
+
+def split_up(array, dim, devices):
+    shape = array.shape
+    tiles = array.reshape(*shape[:dim], devices, shape[dim] // devices, *shape[dim + 1 :])
+    return jnp.moveaxis(tiles, dim, 0)
+
+
+def in_order(blocks, dim):
+    blocks = jnp.moveaxis(blocks, 0, dim)
+    dims = blocks.shape
+    return blocks.reshape(*dims[:dim], dims[dim] * dims[dim + 1], *dims[dim + 2 :])
+
+
+def swapped_with_each(value, axis, split_dim, concat_dim):
+    count, place = (lax.axis_size(axis), lax.axis_index(axis))
+    blocks = split_up(value, split_dim, count)
+    outs = [blocks[place]]
+    for turn in range(1, count):
+        sent = blocks[place ^ turn]
+        outs.append(lax.ppermute(sent, axis, [(i, i ^ turn) for i in range(count)]))
+    blocks = jnp.stack(outs)[place ^ jnp.arange(count)]
+    return in_order(blocks, concat_dim)
 
 
 def padded_2(block, sides, width):
@@ -237,7 +260,7 @@
             )
             disco_out = disco_out + kernel_here[:, :, reach, span][:, :, None] * window
     mixed_field = (spectral + disco_out).astype(jnp.bfloat16)
-    mixed_rows = lax.all_to_all(mixed_field, "chan", split_axis=2, concat_axis=0, tiled=True)
+    mixed_rows = swapped_with_each(mixed_field, "chan", 2, 0)
     all_channels = mixed_rows.shape[0]
     row_width = mixed_rows.shape[2]
     grad_rows, grad_hidden, grad_output = mlp_backward(

time: 487 us -> 512 us (1.051)
  starting transfers between devices: 71.5 us -> 93.8 us
    ppermute x0 -> x7, starting transfers between devices: none -> 26.9 us  [swapped_with_each(): outs.append(lax.ppermute(sent, axis, [(i, i ^ turn) for i in range(count)]))]
    all_to_all x1 -> x0, waiting for transfers between devices: 7.47 us -> none  [shards(): lax.all_to_all(mixed_field, 'chan', split_axis=2, concat_axis=0, tiled=True)]
    all_to_all x1 -> x0, starting transfers between devices: 6.38 us -> none  [shards(): lax.all_to_all(mixed_field, 'chan', split_axis=2, concat_axis=0, tiled=True)]
    all_to_all x1, waiting for transfers between devices: 0.83 us -> 6.93 us  [shards(): lax.all_to_all(adjoint_member, 'chan', split_axis=2, concat_axis=0, tiled...]
  transfers between devices with their start and end apart: 12 -> 18, of which waited for: 4 -> 4; matrix products, arithmetic and copies ran while one was open for 9% -> 8% of each run, Pallas kernels for 0% -> 0%
where the time goes in v1:
time: 512 us; the launch traced here: 511 us
  blocking collectives  277 us (54%)
  starting transfers between devices  93.8 us (18%)
  between operations  57.8 us (11%)
  local copies, waits for them, and re-layouts  25.7 us (5%)
  matrix products  21.8 us (4%)
  waiting for transfers between devices  20 us (4%)
  other arithmetic  14.4 us (3%)
    psum x1, blocking collectives, shards(): lax.psum((filter_part, disco_part), ('ens', 'lat'))  277 us
    ppermute x7, starting transfers between devices, swapped_with_each(): outs.append(lax.ppermute(sent, axis, [(i, i ^ turn) for i in range(count)]))  26.9 us
    all_to_all x2, starting transfers between devices, to_modes(): lax.all_to_all(spectrum, 'lat', split_axis=3, concat_axis=1, tiled=True)  18.5 us
    all_to_all x2, starting transfers between devices, to_bands(): lax.all_to_all(spectrum, 'lat', split_axis=1, concat_axis=3, tiled=True)  17.6 us
    ppermute x2, starting transfers between devices, padded_2(): lax.ppermute(lax.slice_in_dim(block, 0, width, axis=dim), axis, backward)  11.6 us
  transfers between devices with their start and end apart: 18, of which 4 were waited for; matrix products, arithmetic and copies ran while one was open for 8% of the time, Pallas kernels for 0%

profile of v1, /device:TPU:256, one launch (start us, length us, event | category | flops | bytes accessed | tf_op | source)
XLA Modules:
  0.0 510.5 jit_solution(10365059083648567608)
XLA Ops:
  7.5 0.9 reshape_squeeze.3
  8.9 0.8 reshape.55231
  9.7 9.9 %all-to-all-start = ((bf16[32,2,384]{2,1,0:T(2,128)(2,1)}), bf16[32,2,384]{2,1,0:T(2,128)(2,1)S(1)}, u32[]{:S(2)}, u32[]{:S(2)}) async-start(bf16[32,2,384]{2,1,0:T(2,128)(2,1)} %reshape.55231), calls=%async_computation | async-start | bytes 98304 | tf_op jit(solution)/shard_map/all_to_all | solution.py:177
  19.6 3.4 collective-permute-start
  23.0 5.8 %collective-permute-start.1 = (bf16[48,2,256]{2,0,1:T(8,128)(2,1)S(1)}, bf16[48,2,256]{2,0,1:T(8,128)(2,1)S(1)}, u32[]{:S(2)}, u32[]{:S(2)}) collective-permute-start(bf16[48,2,256]{2,0,1:T(8,128)(2,1)S(1)} %get-tuple-element.534), channel_id=1, source_target_pairs={{8,0},{16,8},{24,16},{32,24},{40,32},{48,40},{56,48},{64,56},{72,6... | collective-permute-start | bytes 147464 | tf_op jit(solution)/shard_map/ppermute | solution.py:46
  28.8 0.7 fusion.697
  33.4 0.7 fusion.698
  49.8 0.7 fusion.696
  74.1 0.7 fusion.688
  77.1 0.9 convolution_bitcast_fusion
  79.3 0.7 fusion.685
  86.3 1.0 reshape.55235
  88.4 7.1 %all-to-all-start.2 = ((bf16[8,2,3072]{2,1,0:T(2,128)(2,1)}), bf16[8,2,3072]{2,1,0:T(2,128)(2,1)S(1)}, u32[]{:S(2)}, u32[]{:S(2)}) async-start(bf16[8,2,3072]{2,1,0:T(2,128)(2,1)} %reshape.55235), calls=%async_computation.2 | async-start | bytes 196608 | tf_op jit(solution)/shard_map/all_to_all | solution.py:227
  96.5 0.8 reshape.55233
  97.3 6.9 %all-to-all-done.2 = bf16[8,2,3072]{2,1,0:T(2,128)(2,1)S(1)} async-done(((bf16[8,2,3072]{2,1,0:T(2,128)(2,1)}), bf16[8,2,3072]{2,1,0:T(2,128)(2,1)S(1)}, u32[]{:S(2)}, u32[]{:S(2)}) %all-to-all-start.2) | async-done | bytes 98336 | tf_op jit(solution)/shard_map/all_to_all | solution.py:227
  104.3 7.4 %all-to-all-start.1 = ((bf16[32,2,384]{2,1,0:T(2,128)(2,1)}), bf16[32,2,384]{2,1,0:T(2,128)(2,1)S(1)}, u32[]{:S(2)}, u32[]{:S(2)}) async-start(bf16[32,2,384]{2,1,0:T(2,128)(2,1)} %reshape.55233), calls=%async_computation.1 | async-start | bytes 98304 | tf_op jit(solution)/shard_map/all_to_all | solution.py:181
  112.8 3.9 all-to-all-done.1
  117.5 6.3 %fusion.2 = bf16[48,4,256]{2,0,1:T(8,128)(2,1)S(1)} fusion(bf16[48,4,128]{0,2,1:T(8,128)(2,1)S(1)} %bitcast.640, bf16[48,4,256]{2,0,1:T(8,128)(2,1)S(1)} %bitcast.616, f32[48,4]{0,1:T(4,128)S(1)} %bitcast.853, f32[48,4]{0,1:T(4,128)S(1)} %bitcast.854, f32[48,4]{0,1:T(4,128)S(1)} %bitcast.855, f32[48,4]{0,1:T(4,128)S(1)} %bitcast.856, ...), kind=kOutput, calls=%fused_computation.174 | convolution fusion | flops 25493504 | bytes 8339200 | tf_op jit(solution)/shard_map/dot_general | solution.py:240
  124.0 0.8 constant_dynamic-slice_fusion
  125.0 2.5 collective-permute-start.2
  127.6 2.2 collective-permute-start.3
  129.9 5.4 %collective-permute-start.4 = (bf16[48,4,32]{0,2,1:T(8,128)(2,1)S(1)}, bf16[48,4,32]{0,2,1:T(8,128)(2,1)S(1)}, u32[]{:S(2)}, u32[]{:S(2)}) collective-permute-start(bf16[48,4,32]{0,2,1:T(8,128)(2,1)S(1)} %bitcast.647), channel_id=1, source_target_pairs={{0,3},{1,2},{2,1},{3,0},{4,7},{5,6},{6,5},{7,4},{8,11},{9,10},{10,... | collective-permute-start | bytes 36872 | tf_op jit(solution)/shard_map/ppermute | solution.py:33
  135.5 2.5 collective-permute-start.5
  138.1 5.5 %collective-permute-start.6 = (bf16[48,4,32]{0,2,1:T(8,128)(2,1)S(1)}, bf16[48,4,32]{0,2,1:T(8,128)(2,1)S(1)}, u32[]{:S(2)}, u32[]{:S(2)}) collective-permute-start(bf16[48,4,32]{0,2,1:T(8,128)(2,1)S(1)} %bitcast.645), channel_id=1, source_target_pairs={{0,5},{1,4},{2,7},{3,6},{4,1},{5,0},{6,3},{7,2},{8,13},{9,12},{10,... | collective-permute-start | bytes 36872 | tf_op jit(solution)/shard_map/ppermute | solution.py:33
  143.8 4.1 collective-permute-start.7
  147.9 4.8 collective-permute-start.8
  152.8 2.1 collective-permute-done.8
  156.6 2.0 fusion.24
  159.7 1.0 reshape.55237
  160.8 5.1 %all-to-all-start.3 = ((bf16[8,2,3072]{2,1,0:T(2,128)(2,1)}), bf16[8,2,3072]{2,1,0:T(2,128)(2,1)S(1)}, u32[]{:S(2)}, u32[]{:S(2)}) async-start(bf16[8,2,3072]{2,1,0:T(2,128)(2,1)} %reshape.55237), calls=%async_computation.3 | async-start | bytes 196608 | tf_op jit(solution)/shard_map/all_to_all | solution.py:272
  166.2 1.5 fusion.617
  167.7 7.0 %all-to-all-done.3 = bf16[8,2,3072]{2,1,0:T(2,128)(2,1)S(1)} async-done(((bf16[8,2,3072]{2,1,0:T(2,128)(2,1)}), bf16[8,2,3072]{2,1,0:T(2,128)(2,1)S(1)}, u32[]{:S(2)}, u32[]{:S(2)}) %all-to-all-start.3) | async-done | bytes 98336 | tf_op jit(solution)/shard_map/all_to_all | solution.py:272
  175.9 1.1 fusion.210
  177.0 1.2 fusion.219
  178.2 1.1 fusion.209
  179.3 1.2 fusion.218
  181.2 0.8 reshape.55239
  182.1 8.6 %all-to-all-start.4 = ((bf16[32,2,384]{2,1,0:T(2,128)(2,1)}), bf16[32,2,384]{2,1,0:T(2,128)(2,1)S(1)}, u32[]{:S(2)}, u32[]{:S(2)}) async-start(bf16[32,2,384]{2,1,0:T(2,128)(2,1)} %reshape.55239), calls=%async_computation.4 | async-start | bytes 98304 | tf_op jit(solution)/shard_map/all_to_all | solution.py:177
  190.7 3.4 collective-permute-start.9
  194.1 5.8 %collective-permute-start.10 = (bf16[48,2,256]{2,0,1:T(8,128)(2,1)S(1)}, bf16[48,2,256]{2,0,1:T(8,128)(2,1)S(1)}, u32[]{:S(2)}, u32[]{:S(2)}) collective-permute-start(bf16[48,2,256]{2,0,1:T(8,128)(2,1)S(1)} %get-tuple-element.532), channel_id=1, source_target_pairs={{8,0},{16,8},{24,16},{32,24},{40,32},{48,40},{56,48},{64,56},{72,6... | collective-permute-start | bytes 147464 | tf_op jit(solution)/shard_map/ppermute | solution.py:46
  199.9 0.8 fusion.217
  203.4 0.8 reshape.55241
  204.2 10.2 %all-to-all-start.5 = ((bf16[32,2,384]{2,1,0:T(2,128)(2,1)}), bf16[32,2,384]{2,1,0:T(2,128)(2,1)S(1)}, u32[]{:S(2)}, u32[]{:S(2)}) async-start(bf16[32,2,384]{2,1,0:T(2,128)(2,1)} %reshape.55241), calls=%async_computation.5 | async-start | bytes 98304 | tf_op jit(solution)/shard_map/all_to_all | solution.py:181
  214.4 276.9 %all-reduce.4 = (f32[2,64,48]{1,2,0:T(8,128)}, f32[9,48]{1,0:T(8,128)S(1)}) all-reduce(f32[2,64,48]{1,2,0:T(8,128)S(1)} %pad_maximum_fusion.8, f32[9,48]{1,0:T(8,128)S(1)} %convolution_bitcast_fusion.6), channel_id=1, replica_groups=mesh['ens'=2,'lat'=32,'chan'=8] {'ens','lat'}, use_global_device_ids=true, to_apply=%region_4.5 | all-reduce | flops 6576 | bytes 52608 | tf_op jit(solution)/shard_map/psum | solution.py:343
  492.6 7.4 %fusion.4 = bf16[1,48,4,256]{3,1,2,0:T(8,128)(2,1)S(1)} fusion(bf16[48,4,128]{0,2,1:T(8,128)(2,1)S(1)} %bitcast.639, bf16[48,4,256]{2,0,1:T(8,128)(2,1)S(1)} %all_to_all.92, bf16[48,8,256]{2,0,1:T(8,128)(2,1)S(1)} %get-tuple-element.537, bf16[48,8,8]{2,0,1:T(8,128)(2,1)S(1)} %get-tuple-element.518, bf16[48,8,8]{2,0,1:T(8,128)(2,1)S(1)} %get-tuple-element.517, ...), kind=kOutput, calls=%fused_computation.178 | convolution fusion | flops 37191680 | bytes 1076992 | tf_op jit(solution)/shard_map/dot_general | solution.py:295
  500.1 0.7 copy.275
  500.8 1.5 dynamic-slice_multiply_fusion
  502.3 1.4 dynamic-slice_multiply_fusion.1
  (462 shorter events, 24.5 us)
Async XLA Ops:
  9.7 78.7 %all-to-all-start = ((bf16[32,2,384]{2,1,0:T(2,128)(2,1)}), bf16[32,2,384]{2,1,0:T(2,128)(2,1)S(1)}, u32[]{:S(2)}, u32[]{:S(2)}) async-start(bf16[32,2,384]{2,1,0:T(2,128)(2,1)} %reshape.55231), calls=%async_computation | async-start | bytes 98304 | tf_op jit(solution)/shard_map/all_to_all | solution.py:177
  19.6 68.6 %collective-permute-start = (bf16[48,2,256]{2,0,1:T(8,128)(2,1)S(1)}, bf16[48,2,256]{2,0,1:T(8,128)(2,1)S(1)}, u32[]{:S(2)}, u32[]{:S(2)}) collective-permute-start(bf16[48,2,256]{2,0,1:T(8,128)(2,1)S(1)} %get-tuple-element.535), channel_id=1, source_target_pairs={{0,8},{8,16},{16,24},{24,32},{32,40},{40,48},{48,56},{56,64},{64,7... | collective-permute-start | bytes 147464 | tf_op jit(solution)/shard_map/ppermute | solution.py:43
  23.0 65.3 %collective-permute-start.1 = (bf16[48,2,256]{2,0,1:T(8,128)(2,1)S(1)}, bf16[48,2,256]{2,0,1:T(8,128)(2,1)S(1)}, u32[]{:S(2)}, u32[]{:S(2)}) collective-permute-start(bf16[48,2,256]{2,0,1:T(8,128)(2,1)S(1)} %get-tuple-element.534), channel_id=1, source_target_pairs={{8,0},{16,8},{24,16},{32,24},{40,32},{48,40},{56,48},{64,56},{72,6... | collective-permute-start | bytes 147464 | tf_op jit(solution)/shard_map/ppermute | solution.py:46
  88.4 15.9 %all-to-all-start.2 = ((bf16[8,2,3072]{2,1,0:T(2,128)(2,1)}), bf16[8,2,3072]{2,1,0:T(2,128)(2,1)S(1)}, u32[]{:S(2)}, u32[]{:S(2)}) async-start(bf16[8,2,3072]{2,1,0:T(2,128)(2,1)} %reshape.55235), calls=%async_computation.2 | async-start | bytes 196608 | tf_op jit(solution)/shard_map/all_to_all | solution.py:227
  104.3 12.5 %all-to-all-start.1 = ((bf16[32,2,384]{2,1,0:T(2,128)(2,1)}), bf16[32,2,384]{2,1,0:T(2,128)(2,1)S(1)}, u32[]{:S(2)}, u32[]{:S(2)}) async-start(bf16[32,2,384]{2,1,0:T(2,128)(2,1)} %reshape.55233), calls=%async_computation.1 | async-start | bytes 98304 | tf_op jit(solution)/shard_map/all_to_all | solution.py:181
  125.0 18.7 %collective-permute-start.2 = (bf16[48,4,32]{0,2,1:T(8,128)(2,1)S(1)}, bf16[48,4,32]{0,2,1:T(8,128)(2,1)S(1)}, u32[]{:S(2)}, u32[]{:S(2)}) collective-permute-start(bf16[48,4,32]{0,2,1:T(8,128)(2,1)S(1)} %bitcast.649), channel_id=1, source_target_pairs={{0,1},{1,0},{2,3},{3,2},{4,5},{5,4},{6,7},{7,6},{8,9},{9,8},{10,11... | collective-permute-start | bytes 36872 | tf_op jit(solution)/shard_map/ppermute | solution.py:33
  127.6 20.3 %collective-permute-start.3 = (bf16[48,4,32]{0,2,1:T(8,128)(2,1)S(1)}, bf16[48,4,32]{0,2,1:T(8,128)(2,1)S(1)}, u32[]{:S(2)}, u32[]{:S(2)}) collective-permute-start(bf16[48,4,32]{0,2,1:T(8,128)(2,1)S(1)} %bitcast.648), channel_id=1, source_target_pairs={{0,2},{1,3},{2,0},{3,1},{4,6},{5,7},{6,4},{7,5},{8,10},{9,11},{10,... | collective-permute-start | bytes 36872 | tf_op jit(solution)/shard_map/ppermute | solution.py:33
  129.9 22.7 %collective-permute-start.4 = (bf16[48,4,32]{0,2,1:T(8,128)(2,1)S(1)}, bf16[48,4,32]{0,2,1:T(8,128)(2,1)S(1)}, u32[]{:S(2)}, u32[]{:S(2)}) collective-permute-start(bf16[48,4,32]{0,2,1:T(8,128)(2,1)S(1)} %bitcast.647), channel_id=1, source_target_pairs={{0,3},{1,2},{2,1},{3,0},{4,7},{5,6},{6,5},{7,4},{8,11},{9,10},{10,... | collective-permute-start | bytes 36872 | tf_op jit(solution)/shard_map/ppermute | solution.py:33
  135.5 17.2 %collective-permute-start.5 = (bf16[48,4,32]{0,2,1:T(8,128)(2,1)S(1)}, bf16[48,4,32]{0,2,1:T(8,128)(2,1)S(1)}, u32[]{:S(2)}, u32[]{:S(2)}) collective-permute-start(bf16[48,4,32]{0,2,1:T(8,128)(2,1)S(1)} %bitcast.646), channel_id=1, source_target_pairs={{0,4},{1,5},{2,6},{3,7},{4,0},{5,1},{6,2},{7,3},{8,12},{9,13},{10,... | collective-permute-start | bytes 36872 | tf_op jit(solution)/shard_map/ppermute | solution.py:33
  138.1 14.7 %collective-permute-start.6 = (bf16[48,4,32]{0,2,1:T(8,128)(2,1)S(1)}, bf16[48,4,32]{0,2,1:T(8,128)(2,1)S(1)}, u32[]{:S(2)}, u32[]{:S(2)}) collective-permute-start(bf16[48,4,32]{0,2,1:T(8,128)(2,1)S(1)} %bitcast.645), channel_id=1, source_target_pairs={{0,5},{1,4},{2,7},{3,6},{4,1},{5,0},{6,3},{7,2},{8,13},{9,12},{10,... | collective-permute-start | bytes 36872 | tf_op jit(solution)/shard_map/ppermute | solution.py:33
  143.8 9.0 %collective-permute-start.7 = (bf16[48,4,32]{0,2,1:T(8,128)(2,1)S(1)}, bf16[48,4,32]{0,2,1:T(8,128)(2,1)S(1)}, u32[]{:S(2)}, u32[]{:S(2)}) collective-permute-start(bf16[48,4,32]{0,2,1:T(8,128)(2,1)S(1)} %bitcast.644), channel_id=1, source_target_pairs={{0,6},{1,7},{2,4},{3,5},{4,2},{5,3},{6,0},{7,1},{8,14},{9,15},{10,... | collective-permute-start | bytes 36872 | tf_op jit(solution)/shard_map/ppermute | solution.py:33
  147.9 7.0 %collective-permute-start.8 = (bf16[48,4,32]{0,2,1:T(8,128)(2,1)S(1)}, bf16[48,4,32]{0,2,1:T(8,128)(2,1)S(1)}, u32[]{:S(2)}, u32[]{:S(2)}) collective-permute-start(bf16[48,4,32]{0,2,1:T(8,128)(2,1)S(1)} %bitcast.643), channel_id=1, source_target_pairs={{0,7},{1,6},{2,5},{3,4},{4,3},{5,2},{6,1},{7,0},{8,15},{9,14},{10,... | collective-permute-start | bytes 36872 | tf_op jit(solution)/shard_map/ppermute | solution.py:33
  160.8 13.9 %all-to-all-start.3 = ((bf16[8,2,3072]{2,1,0:T(2,128)(2,1)}), bf16[8,2,3072]{2,1,0:T(2,128)(2,1)S(1)}, u32[]{:S(2)}, u32[]{:S(2)}) async-start(bf16[8,2,3072]{2,1,0:T(2,128)(2,1)} %reshape.55237), calls=%async_computation.3 | async-start | bytes 196608 | tf_op jit(solution)/shard_map/all_to_all | solution.py:272
  165.9 334.9 %all-reduce.7.cloned.1.call-start = ((), (), s32[]{:S(2)}) async-start(), calls=%async_computation.6 | async-start | bytes 4718592 | tf_op jit(solution)/shard_map/psum | solution.py:344
  182.1 19.9 %all-to-all-start.4 = ((bf16[32,2,384]{2,1,0:T(2,128)(2,1)}), bf16[32,2,384]{2,1,0:T(2,128)(2,1)S(1)}, u32[]{:S(2)}, u32[]{:S(2)}) async-start(bf16[32,2,384]{2,1,0:T(2,128)(2,1)} %reshape.55239), calls=%async_computation.4 | async-start | bytes 98304 | tf_op jit(solution)/shard_map/all_to_all | solution.py:177
  190.7 11.1 %collective-permute-start.9 = (bf16[48,2,256]{2,0,1:T(8,128)(2,1)S(1)}, bf16[48,2,256]{2,0,1:T(8,128)(2,1)S(1)}, u32[]{:S(2)}, u32[]{:S(2)}) collective-permute-start(bf16[48,2,256]{2,0,1:T(8,128)(2,1)S(1)} %get-tuple-element.533), channel_id=1, source_target_pairs={{0,8},{8,16},{16,24},{24,32},{32,40},{40,48},{48,56},{56,64},{64,7... | collective-permute-start | bytes 147464 | tf_op jit(solution)/shard_map/ppermute | solution.py:43
  194.1 7.8 %collective-permute-start.10 = (bf16[48,2,256]{2,0,1:T(8,128)(2,1)S(1)}, bf16[48,2,256]{2,0,1:T(8,128)(2,1)S(1)}, u32[]{:S(2)}, u32[]{:S(2)}) collective-permute-start(bf16[48,2,256]{2,0,1:T(8,128)(2,1)S(1)} %get-tuple-element.532), channel_id=1, source_target_pairs={{8,0},{16,8},{24,16},{32,24},{40,32},{48,40},{56,48},{64,56},{72,6... | collective-permute-start | bytes 147464 | tf_op jit(solution)/shard_map/ppermute | solution.py:46
  202.6 289.7 %copy-start.7 = (f32[48,4,1,1]{0,3,2,1:T(1,128)S(1)}, f32[48,4,1,1]{0,3,2,1:T(1,128)}, u32[]{:S(2)}) copy-start(f32[48,4,1,1]{0,3,2,1:T(1,128)} %get-tuple-element.371) | copy-start | bytes 2308
  202.6 289.7 %copy-start.8 = (f32[48,4,1,1]{0,3,2,1:T(1,128)S(1)}, f32[48,4,1,1]{0,3,2,1:T(1,128)}, u32[]{:S(2)}) copy-start(f32[48,4,1,1]{0,3,2,1:T(1,128)} %get-tuple-element.372) | copy-start | bytes 2308
  202.6 289.7 %copy-start.9 = (f32[48,4,1,1]{0,3,2,1:T(1,128)S(1)}, f32[48,4,1,1]{0,3,2,1:T(1,128)}, u32[]{:S(2)}) copy-start(f32[48,4,1,1]{0,3,2,1:T(1,128)} %get-tuple-element.373) | copy-start | bytes 2308
  202.6 289.7 %copy-start.10 = (f32[48,4,1,1]{0,3,2,1:T(1,128)S(1)}, f32[48,4,1,1]{0,3,2,1:T(1,128)}, u32[]{:S(2)}) copy-start(f32[48,4,1,1]{0,3,2,1:T(1,128)} %get-tuple-element.374) | copy-start | bytes 2308
  202.6 289.7 %copy-start.11 = (f32[48,4,1,1]{0,3,2,1:T(1,128)S(1)}, f32[48,4,1,1]{0,3,2,1:T(1,128)}, u32[]{:S(2)}) copy-start(f32[48,4,1,1]{0,3,2,1:T(1,128)} %get-tuple-element.375) | copy-start | bytes 2308
  202.6 289.7 %copy-start.12 = (f32[48,4,1,1]{0,3,2,1:T(1,128)S(1)}, f32[48,4,1,1]{0,3,2,1:T(1,128)}, u32[]{:S(2)}) copy-start(f32[48,4,1,1]{0,3,2,1:T(1,128)} %get-tuple-element.376) | copy-start | bytes 2308
  202.6 289.7 %copy-start.13 = (f32[48,4,1,1]{0,3,2,1:T(1,128)S(1)}, f32[48,4,1,1]{0,3,2,1:T(1,128)}, u32[]{:S(2)}) copy-start(f32[48,4,1,1]{0,3,2,1:T(1,128)} %get-tuple-element.377) | copy-start | bytes 2308
  202.6 289.7 %copy-start.14 = (f32[48,4,1,1]{0,3,2,1:T(1,128)S(1)}, f32[48,4,1,1]{0,3,2,1:T(1,128)}, u32[]{:S(2)}) copy-start(f32[48,4,1,1]{0,3,2,1:T(1,128)} %get-tuple-element.378) | copy-start | bytes 2308
  202.6 289.7 %copy-start.15 = (f32[48,4,1,1]{0,3,2,1:T(1,128)S(1)}, f32[48,4,1,1]{0,3,2,1:T(1,128)}, u32[]{:S(2)}) copy-start(f32[48,4,1,1]{0,3,2,1:T(1,128)} %get-tuple-element.379) | copy-start | bytes 2308
  202.7 289.7 %copy-start.16 = (f32[48,4,1,1]{0,3,2,1:T(1,128)S(1)}, f32[48,4,1,1]{0,3,2,1:T(1,128)}, u32[]{:S(2)}) copy-start(f32[48,4,1,1]{0,3,2,1:T(1,128)} %get-tuple-element.380) | copy-start | bytes 2308
  202.7 289.7 %copy-start.17 = (f32[48,4,1,1]{0,3,2,1:T(1,128)S(1)}, f32[48,4,1,1]{0,3,2,1:T(1,128)}, u32[]{:S(2)}) copy-start(f32[48,4,1,1]{0,3,2,1:T(1,128)} %get-tuple-element.381) | copy-start | bytes 2308
  202.7 289.7 %copy-start.18 = (f32[48,4,1,1]{0,3,2,1:T(1,128)S(1)}, f32[48,4,1,1]{0,3,2,1:T(1,128)}, u32[]{:S(2)}) copy-start(f32[48,4,1,1]{0,3,2,1:T(1,128)} %get-tuple-element.382) | copy-start | bytes 2308
  202.7 289.7 %copy-start.19 = (f32[48,4,1,1]{0,3,2,1:T(1,128)S(1)}, f32[48,4,1,1]{0,3,2,1:T(1,128)}, u32[]{:S(2)}) copy-start(f32[48,4,1,1]{0,3,2,1:T(1,128)} %get-tuple-element.383) | copy-start | bytes 2308
  202.7 289.7 %copy-start.20 = (f32[48,4,1,1]{0,3,2,1:T(1,128)S(1)}, f32[48,4,1,1]{0,3,2,1:T(1,128)}, u32[]{:S(2)}) copy-start(f32[48,4,1,1]{0,3,2,1:T(1,128)} %get-tuple-element.384) | copy-start | bytes 2308
  202.7 289.7 %copy-start.21 = (f32[48,4,1,1]{0,3,2,1:T(1,128)S(1)}, f32[48,4,1,1]{0,3,2,1:T(1,128)}, u32[]{:S(2)}) copy-start(f32[48,4,1,1]{0,3,2,1:T(1,128)} %get-tuple-element.385) | copy-start | bytes 2308
  202.7 289.7 %copy-start.22 = (f32[48,4,1,1]{0,3,2,1:T(1,128)S(1)}, f32[48,4,1,1]{0,3,2,1:T(1,128)}, u32[]{:S(2)}) copy-start(f32[48,4,1,1]{0,3,2,1:T(1,128)} %get-tuple-element.386) | copy-start | bytes 2308
  202.7 289.7 %copy-start.23 = (f32[48,4,1,1]{0,3,2,1:T(1,128)S(1)}, f32[48,4,1,1]{0,3,2,1:T(1,128)}, u32[]{:S(2)}) copy-start(f32[48,4,1,1]{0,3,2,1:T(1,128)} %get-tuple-element.387) | copy-start | bytes 2308
  202.7 289.7 %copy-start.24 = (f32[48,4,1,1]{0,3,2,1:T(1,128)S(1)}, f32[48,4,1,1]{0,3,2,1:T(1,128)}, u32[]{:S(2)}) copy-start(f32[48,4,1,1]{0,3,2,1:T(1,128)} %get-tuple-element.388) | copy-start | bytes 2308
  202.7 289.7 %copy-start.25 = (f32[48,4,1,1]{0,3,2,1:T(1,128)S(1)}, f32[48,4,1,1]{0,3,2,1:T(1,128)}, u32[]{:S(2)}) copy-start(f32[48,4,1,1]{0,3,2,1:T(1,128)} %get-tuple-element.389) | copy-start | bytes 2308
  202.8 289.7 %copy-start.26 = (f32[48,4,1,1]{0,3,2,1:T(1,128)S(1)}, f32[48,4,1,1]{0,3,2,1:T(1,128)}, u32[]{:S(2)}) copy-start(f32[48,4,1,1]{0,3,2,1:T(1,128)} %get-tuple-element.390) | copy-start | bytes 2308
  202.8 289.7 %copy-start.27 = (f32[48,4,1,1]{0,3,2,1:T(1,128)S(1)}, f32[48,4,1,1]{0,3,2,1:T(1,128)}, u32[]{:S(2)}) copy-start(f32[48,4,1,1]{0,3,2,1:T(1,128)} %get-tuple-element.391) | copy-start | bytes 2308
  202.8 289.7 %copy-start.28 = (f32[48,4,1,1]{0,3,2,1:T(1,128)S(1)}, f32[48,4,1,1]{0,3,2,1:T(1,128)}, u32[]{:S(2)}) copy-start(f32[48,4,1,1]{0,3,2,1:T(1,128)} %get-tuple-element.392) | copy-start | bytes 2308
  202.8 289.7 %copy-start.29 = (f32[48,4,1,1]{0,3,2,1:T(1,128)S(1)}, f32[48,4,1,1]{0,3,2,1:T(1,128)}, u32[]{:S(2)}) copy-start(f32[48,4,1,1]{0,3,2,1:T(1,128)} %get-tuple-element.393) | copy-start | bytes 2308
  202.8 289.7 %copy-start.30 = (f32[48,4,1,1]{0,3,2,1:T(1,128)S(1)}, f32[48,4,1,1]{0,3,2,1:T(1,128)}, u32[]{:S(2)}) copy-start(f32[48,4,1,1]{0,3,2,1:T(1,128)} %get-tuple-element.394) | copy-start | bytes 2308
  202.8 289.7 %copy-start.31 = (f32[48,4,1,1]{0,3,2,1:T(1,128)S(1)}, f32[48,4,1,1]{0,3,2,1:T(1,128)}, u32[]{:S(2)}) copy-start(f32[48,4,1,1]{0,3,2,1:T(1,128)} %get-tuple-element.395) | copy-start | bytes 2308
  202.8 289.7 %copy-start.32 = (f32[48,4,1,1]{0,3,2,1:T(1,128)S(1)}, f32[48,4,1,1]{0,3,2,1:T(1,128)}, u32[]{:S(2)}) copy-start(f32[48,4,1,1]{0,3,2,1:T(1,128)} %get-tuple-element.396) | copy-start | bytes 2308
  202.8 289.7 %copy-start.33 = (f32[48,4,1,1]{0,3,2,1:T(1,128)S(1)}, f32[48,4,1,1]{0,3,2,1:T(1,128)}, u32[]{:S(2)}) copy-start(f32[48,4,1,1]{0,3,2,1:T(1,128)} %get-tuple-element.397) | copy-start | bytes 2308
  202.8 289.7 %copy-start.34 = (f32[48,4,1,1]{0,3,2,1:T(1,128)S(1)}, f32[48,4,1,1]{0,3,2,1:T(1,128)}, u32[]{:S(2)}) copy-start(f32[48,4,1,1]{0,3,2,1:T(1,128)} %get-tuple-element.398) | copy-start | bytes 2308
  202.8 289.7 %copy-start.35 = (f32[48,4,1,1]{0,3,2,1:T(1,128)S(1)}, f32[48,4,1,1]{0,3,2,1:T(1,128)}, u32[]{:S(2)}) copy-start(f32[48,4,1,1]{0,3,2,1:T(1,128)} %get-tuple-element.399) | copy-start | bytes 2308
  202.9 289.7 %copy-start.36 = (f32[48,4,1,1]{0,3,2,1:T(1,128)S(1)}, f32[48,4,1,1]{0,3,2,1:T(1,128)}, u32[]{:S(2)}) copy-start(f32[48,4,1,1]{0,3,2,1:T(1,128)} %get-tuple-element.400) | copy-start | bytes 2308
  204.2 287.7 %all-to-all-start.5 = ((bf16[32,2,384]{2,1,0:T(2,128)(2,1)}), bf16[32,2,384]{2,1,0:T(2,128)(2,1)S(1)}, u32[]{:S(2)}, u32[]{:S(2)}) async-start(bf16[32,2,384]{2,1,0:T(2,128)(2,1)} %reshape.55241), calls=%async_computation.5 | async-start | bytes 98304 | tf_op jit(solution)/shard_map/all_to_all | solution.py:181
  (59 other events, 3545.6 us)
Sparse Core Ops, SparseCore 0:
  171.8 280.0 all-reduce.6
